TPU v7x, 32 devices: a whole 2x2x4 slice. The times are simulated.
32 devices in a mesh: freq: 16 (over z, x, core), mz: 2 (over y).
Axes of the slice: x: 2, y: 2, z: 4, core: 2. Of those that a mesh axis runs over, the one named last changes fastest.
Arguments:
- intensity: bfloat16 [8, 6144, 4096], P(None, 'freq', 'mz'), may hold values from -6 to 6
- elution: float32 [6144, 64], P(('freq', 'mz')), may hold values from -6 to 6
- loadings: float32 [8, 64], replicated, may hold values from 0.0005 to 0.01
- shifts: int32 [8, 64], replicated, may hold values from 0 to 255
- bin_weight: float32 [6144], replicated, may hold values from 0.25 to 4
Outputs:
- spectral: float32 [64, 4096], P(None, ('mz', 'freq'))
All inputs are finite; a program needn't handle non-finite values.
Results may differ from a plain program's by a relative error of at most 0.0003.
Values may be sent and summed in bfloat16 or wider, within the bound.
No kernel may reach another device: no remote copies, remote signals or barrier semaphores. Data moves between devices by JAX's collectives and lax.ppermute only.
A program may use at most 64 MiB of HBM per device.

v0:
```python
import math

import jax
import jax.numpy as jnp
from jax import lax
from jax.sharding import PartitionSpec as P

PRECISE = lax.Precision.HIGHEST


def turn_angle(product, length):
    return 2.0 * math.pi / length * (product % length).astype(jnp.float32)


def cholesky_solve(gram_matrix, numerator):
    factor = jnp.linalg.cholesky(gram_matrix)
    middle = lax.linalg.triangular_solve(factor, numerator, left_side=True, lower=True)
    return lax.linalg.triangular_solve(factor, middle, left_side=True, lower=True, transpose_a=True)


def on_device(intensity, elution, loadings, shifts, bin_weight):
    freq_count = lax.axis_size("freq")
    mz_count = lax.axis_size("mz")
    freq_rank = lax.axis_index("freq")
    mz_rank = lax.axis_index("mz")
    run_count, bin_count, local_mz = intensity.shape
    length = bin_count * freq_count
    components = loadings.shape[1]
    norm_scale = 1.0 / math.sqrt(length)
    dev_ids = jnp.arange(freq_count, dtype=jnp.int32)
    bin_ids = jnp.arange(bin_count, dtype=jnp.int32)
    dev_angle = turn_angle(dev_ids[:, None] * dev_ids[None, :], freq_count)
    cos_dev = jnp.cos(dev_angle)
    sin_dev = jnp.sin(dev_angle)
    bin_angle = turn_angle(bin_ids[:, None] * bin_ids[None, :], bin_count)
    cos_bin = jnp.cos(bin_angle)
    sin_bin = jnp.sin(bin_angle)
    full_elution = lax.all_gather(elution, ("freq", "mz"), axis=0, tiled=True)
    stacked = full_elution.reshape(freq_count, bin_count, components)
    weights_grid = bin_weight.reshape(bin_count, freq_count)
    weights_mine = lax.dynamic_slice_in_dim(weights_grid, freq_rank, 1, 1)[:, 0]
    bins_mine = freq_rank + freq_count * bin_ids
    row_angle = turn_angle(freq_rank * dev_ids, freq_count)
    part_re = jnp.einsum("p,pqr->qr", jnp.cos(row_angle), stacked, precision=PRECISE)
    part_im = -jnp.einsum("p,pqr->qr", jnp.sin(row_angle), stacked, precision=PRECISE)
    own_twid = turn_angle(freq_rank * bin_ids, length)[:, None]
    turn_re = part_re * jnp.cos(own_twid) + part_im * jnp.sin(own_twid)
    turn_im = part_im * jnp.cos(own_twid) - part_re * jnp.sin(own_twid)
    own_re = (
        jnp.dot(cos_bin, turn_re, precision=PRECISE) + jnp.dot(sin_bin, turn_im, precision=PRECISE)
    ) * norm_scale
    own_im = (
        jnp.dot(cos_bin, turn_im, precision=PRECISE) - jnp.dot(sin_bin, turn_re, precision=PRECISE)
    ) * norm_scale
    weights_col = weights_mine[None, :, None]
    weights_full = weights_grid.T[None, :, :, None]
    freq_index = dev_ids[:, None] + freq_count * bin_ids[None, :]
    group_size = 4
    blocks = run_count // group_size

    def weighted_model(grid_re, grid_im, run_amp, run_lag):
        phase = turn_angle(freq_index[None, :, :, None] * run_lag[:, None, None, :], length)
        phase_cos = jnp.cos(phase)
        phase_sin = jnp.sin(phase)
        amp_full = run_amp[:, None, None, :]
        wmod_re = weights_full * amp_full * (grid_re * phase_cos + grid_im * phase_sin)
        wmod_im = weights_full * amp_full * (grid_im * phase_cos - grid_re * phase_sin)
        return (wmod_re, wmod_im)

    all_re = jnp.einsum("ap,pqr->aqr", cos_dev, stacked, precision=PRECISE)
    all_im = -jnp.einsum("ap,pqr->aqr", sin_dev, stacked, precision=PRECISE)
    full_twid = turn_angle(dev_ids[:, None] * bin_ids[None, :], length)[:, :, None]
    rot_re = all_re * jnp.cos(full_twid) + all_im * jnp.sin(full_twid)
    rot_im = all_im * jnp.cos(full_twid) - all_re * jnp.sin(full_twid)
    model_grid_re = (
        jnp.einsum("bq,aqr->abr", cos_bin, rot_re, precision=PRECISE)
        + jnp.einsum("bq,aqr->abr", sin_bin, rot_im, precision=PRECISE)
    ) * norm_scale
    model_grid_im = (
        jnp.einsum("bq,aqr->abr", cos_bin, rot_im, precision=PRECISE)
        - jnp.einsum("bq,aqr->abr", sin_bin, rot_re, precision=PRECISE)
    ) * norm_scale
    grid_re = model_grid_re
    grid_im = model_grid_im
    scan_times = freq_rank * bin_count + bin_ids
    flat_freq = freq_index.reshape(length)
    scan_angle = turn_angle(flat_freq[:, None] * scan_times[None, :], length)
    cos_scan = jnp.cos(scan_angle)
    sin_scan = jnp.sin(scan_angle)

    def fold_scans(summed, inputs):
        block_data, run_amp, run_lag = inputs
        wmod_re, wmod_im = weighted_model(grid_re, grid_im, run_amp, run_lag)
        flat_re = wmod_re.reshape(group_size, length, components)
        flat_im = wmod_im.reshape(group_size, length, components)
        kernel = jnp.einsum("gfr,fj->gjr", flat_re, cos_scan, precision=PRECISE) - jnp.einsum(
            "gfr,fj->gjr", flat_im, sin_scan, precision=PRECISE
        )
        increment = jnp.einsum(
            "gjr,gjm->rm", kernel, block_data.astype(jnp.float32), precision=PRECISE
        )
        return (summed + increment, None)

    scanned = (
        intensity.reshape(blocks, group_size, bin_count, local_mz),
        loadings.reshape(blocks, group_size, components),
        shifts.reshape(blocks, group_size, components),
    )
    numerator, _ = lax.scan(fold_scans, jnp.zeros((components, local_mz), jnp.float32), scanned)
    numerator = numerator * norm_scale
    run_share = run_count // mz_count
    run_amp = lax.dynamic_slice_in_dim(loadings, mz_rank * run_share, run_share, 0)
    run_lag = lax.dynamic_slice_in_dim(shifts, mz_rank * run_share, run_share, 0)
    phase = turn_angle(bins_mine[None, :, None] * run_lag[:, None, :], length)
    phase_cos = jnp.cos(phase)
    phase_sin = jnp.sin(phase)
    model_re = run_amp[:, None, :] * (own_re * phase_cos + own_im * phase_sin)
    model_im = run_amp[:, None, :] * (own_im * phase_cos - own_re * phase_sin)
    model_re, model_im = (model_re, model_im)
    gram_matrix = lax.psum(
        jnp.einsum("kbr,kbs->rs", weights_col * model_re, model_re, precision=PRECISE)
        + jnp.einsum("kbr,kbs->rs", weights_col * model_im, model_im, precision=PRECISE),
        ("freq", "mz"),
    )
    owned = lax.psum_scatter(numerator, "freq", scatter_dimension=1, tiled=True)
    return cholesky_solve(gram_matrix, owned)


def solution(mesh):
    in_specs = (P(None, "freq", "mz"), P(("freq", "mz"), None), P(), P(), P())
    out_specs = P(None, ("mz", "freq"))
    return jax.shard_map(
        on_device, mesh=mesh, in_specs=in_specs, out_specs=out_specs, check_vma=False
    )
```

profile of v0, /device:TPU:0, one launch (start us, length us, event | category | flops | bytes accessed | tf_op | source)
XLA Modules:
  0.0 579.2 jit_solution(17927646738032027337)
XLA Ops:
  6.5 0.7 all-gather.3.cloned.1.call-update
  7.3 0.0 reduce-scatter.2.cloned.1.call-start
  7.3 0.8 reshape.148
  8.2 0.7 copy.34
  8.9 0.6 add.224
  9.5 0.8 dynamic-slice_reduce_fusion
  10.3 0.6 broadcast_add_fusion
  10.9 1.3 constant_dynamic-slice_fusion
  12.2 1.3 constant_dynamic-slice_fusion.1
  13.5 0.1 fusion.212
  13.5 0.1 fusion.191
  13.7 56.0 %all-gather.3.cloned.1.call-done = f32[32,192,64]{1,2,0:T(8,128)} async-done(((f32[1,192,64]{1,2,0:T(8,128)}), f32[32,192,64]{1,2,0:T(8,128)}) %all-gather.3.cloned.1.call-update) | async-done | bytes 1572880 | tf_op jit(solution)/shard_map/all_gather | solution.py:38
  69.7 4.1 copy.26
  73.8 2.3 reshape.149
  76.1 0.9 fusion.231
  77.0 0.9 fusion.229
  77.8 0.1 copy.37
  78.0 0.1 copy.38
  78.1 3.0 fusion.109
  81.2 3.0 fusion.111
  84.2 1.5 convolution_negate_fusion
  85.7 3.9 fusion.92
  89.6 3.7 fusion.93
  93.2 1.8 multiply_subtract_fusion
  95.0 5.6 fusion.86
  100.6 5.8 %fusion.90 = f32[16,64,384]{2,1,0:T(8,128)S(1)} fusion(f32[16,384,64]{1,0,2:T(8,128)S(1)} %get-tuple-element.312), kind=kOutput, calls=%fused_computation.83 | convolution fusion | flops 1813266432 | bytes 3145728 | tf_op jit(solution)/shard_map/bq,aqr->abr/dot_general | solution.py:76
  106.5 5.7 multiply_bitcast_fusion
  112.1 0.9 copy.36
  113.1 5.9 %multiply_bitcast_fusion.1 = f32[16,384,64]{1,2,0:T(8,128)S(1)} fusion(f32[16,64,384]{2,1,0:T(8,128)S(1)} %fusion.90, f32[16,384,64]{1,0,2:T(8,128)S(1)} %get-tuple-element.311), kind=kOutput, calls=%fused_computation.75 | convolution fusion | flops 1814052864 | bytes 4718592 | tf_op jit(solution)/shard_map/bq,aqr->abr/dot_general | solution.py:77
  119.0 0.9 copy.35
  119.9 388.7 %while.15 = (s32[]{:T(128)}, f32[64,2048]{1,0:T(8,128)}, f32[1,16,384,1]{2,3,1,0:T(1,128)}, f32[2,4,64]{2,1,0:T(4,128)}, f32[16,384,64]{1,0,2:T(8,128)S(1)}, /*i...) while((s32[]{:T(128)}, f32[64,2048]{1,0:T(8,128)}, ...), condition=%wide.region_4.5_spmd.clone.clone.clone, body=%wide.region_3.4_spmd.clone.clone.clone.sunk | while | flops 16998307840 | bytes 72160480 | solution.py:109
  120.4 0.7 dynamic-slice_bitcast_fusion.4
  121.1 0.7 dynamic-slice_bitcast_fusion.5
  121.8 39.0 %fusion.305 = f32[6144,384,1]{1,0,2:T(8,128)} fusion(s32[384]{0:T(512)S(1)} %get-tuple-element.419, s32[6144]{0:T(1024)} %get-tuple-element.420), kind=kLoop, calls=%fused_computation.8.clone.2.clone.1 | loop fusion | flops 21233664 | bytes 9463296 | tf_op jit(solution)/shard_map/while/body/eval_jaxpr/gfr,fj->gjr/dot_general | solution.py:96
  160.8 1.6 copy.55
  162.4 1.6 copy.56
  164.0 53.1 %fusion.306 = f32[4,64,384]{2,1,0:T(8,128)S(1)} fusion(f32[6144,64]{0,1:T(8,128)} %bitcast.163, s32[4,64]{1,0:T(4,128)S(1)} %dynamic-slice_bitcast_fusion.4, s32[6144]{0:T(1024)S(1)} %mul.1890, f32[6144,64]{0,1:T(8,128)} %bitcast.165, f32[4,64]{1,0:T(4,128)S(1)} %dynamic-slice_bitcast_fusion.5, f32[6144]{0:T(1024)} %bitcast.159, ...), kind=kOutput, calls=%fused_computation.7.clone.3 | convolution fusion | flops 7269777408 | bytes 13027328 | tf_op jit(solution)/shard_map/while/body/eval_jaxpr/gfr,fj->gjr/dot_general | solution.py:96
  217.2 0.0 copy-done.2
  217.2 0.0 copy-start
  217.2 36.8 %fusion.307 = f32[6144,384,1]{1,0,2:T(8,128)S(1)} fusion(s32[384]{0:T(512)S(1)} %get-tuple-element.419, s32[6144]{0:T(1024)} %get-tuple-element.420), kind=kLoop, calls=%fused_computation.10.clone.clone.clone.clone.clone.2.clone.1 | loop fusion | flops 21233664 | bytes 9463296 | tf_op jit(solution)/shard_map/while/body/eval_jaxpr/gfr,fj->gjr/dot_general | solution.py:96
  254.1 50.0 %fusion.308 = f32[4,384,64]{1,2,0:T(8,128)S(1)} fusion(f32[4,64,384]{2,1,0:T(8,128)S(1)} %fusion.306, f32[6144,64]{0,1:T(8,128)S(1)} %bitcast.164, s32[4,64]{1,0:T(4,128)S(1)} %dynamic-slice_bitcast_fusion.4, s32[6144]{0:T(1024)} %copy-done.2, f32[6144,64]{0,1:T(8,128)S(1)} %bitcast.166, f32[4,64]{1,0:T(4,128)S(1)} %dynamic-slice_bitcast_fusion.5, ...), kind=kOutput, calls=%fused_computation.63.clone.3 | convolution fusion | flops 7269875712 | bytes 13420544 | tf_op jit(solution)/shard_map/while/body/eval_jaxpr/gfr,fj->gjr/dot_general | solution.py:96
  304.1 6.3 %fusion.309 = f32[64,2048]{1,0:T(8,128)} fusion(f32[4,384,64]{1,2,0:T(8,128)S(1)} %fusion.308, bf16[2,4,384,2048]{3,2,1,0:T(8,128)(2,1)} %get-tuple-element.417, s32[]{:T(128)} %get-tuple-element.397, f32[64,2048]{1,0:T(8,128)} %get-tuple-element.398, pred[]{:T(512)S(6)} %compare.19), kind=kOutput, calls=%fused_computation.61.clone.1 | convolution fusion | flops 2416181248 | bytes 7733761 | tf_op jit(solution)/shard_map/while/body/eval_jaxpr/gjr,gjm->rm/dot_general | solution.py:99
  310.6 0.7 dynamic-slice_bitcast_fusion.4
  311.3 0.7 dynamic-slice_bitcast_fusion.5
  312.0 39.0 %fusion.305 = f32[6144,384,1]{1,0,2:T(8,128)} fusion(s32[384]{0:T(512)S(1)} %get-tuple-element.419, s32[6144]{0:T(1024)} %get-tuple-element.420), kind=kLoop, calls=%fused_computation.8.clone.2.clone.1 | loop fusion | flops 21233664 | bytes 9463296 | tf_op jit(solution)/shard_map/while/body/eval_jaxpr/gfr,fj->gjr/dot_general | solution.py:96
  351.0 1.6 copy.55
  352.6 1.6 copy.56
  354.3 53.4 %fusion.306 = f32[4,64,384]{2,1,0:T(8,128)S(1)} fusion(f32[6144,64]{0,1:T(8,128)} %bitcast.163, s32[4,64]{1,0:T(4,128)S(1)} %dynamic-slice_bitcast_fusion.4, s32[6144]{0:T(1024)S(1)} %mul.1890, f32[6144,64]{0,1:T(8,128)} %bitcast.165, f32[4,64]{1,0:T(4,128)S(1)} %dynamic-slice_bitcast_fusion.5, f32[6144]{0:T(1024)} %bitcast.159, ...), kind=kOutput, calls=%fused_computation.7.clone.3 | convolution fusion | flops 7269777408 | bytes 13027328 | tf_op jit(solution)/shard_map/while/body/eval_jaxpr/gfr,fj->gjr/dot_general | solution.py:96
  407.7 36.6 %fusion.307 = f32[6144,384,1]{1,0,2:T(8,128)S(1)} fusion(s32[384]{0:T(512)S(1)} %get-tuple-element.419, s32[6144]{0:T(1024)} %get-tuple-element.420), kind=kLoop, calls=%fused_computation.10.clone.clone.clone.clone.clone.2.clone.1 | loop fusion | flops 21233664 | bytes 9463296 | tf_op jit(solution)/shard_map/while/body/eval_jaxpr/gfr,fj->gjr/dot_general | solution.py:96
  444.3 50.0 %fusion.308 = f32[4,384,64]{1,2,0:T(8,128)S(1)} fusion(f32[4,64,384]{2,1,0:T(8,128)S(1)} %fusion.306, f32[6144,64]{0,1:T(8,128)S(1)} %bitcast.164, s32[4,64]{1,0:T(4,128)S(1)} %dynamic-slice_bitcast_fusion.4, s32[6144]{0:T(1024)} %copy-done.2, f32[6144,64]{0,1:T(8,128)S(1)} %bitcast.166, f32[4,64]{1,0:T(4,128)S(1)} %dynamic-slice_bitcast_fusion.5, ...), kind=kOutput, calls=%fused_computation.63.clone.3 | convolution fusion | flops 7269875712 | bytes 13420544 | tf_op jit(solution)/shard_map/while/body/eval_jaxpr/gfr,fj->gjr/dot_general | solution.py:96
  494.3 6.4 %fusion.309 = f32[64,2048]{1,0:T(8,128)} fusion(f32[4,384,64]{1,2,0:T(8,128)S(1)} %fusion.308, bf16[2,4,384,2048]{3,2,1,0:T(8,128)(2,1)} %get-tuple-element.417, s32[]{:T(128)} %get-tuple-element.397, f32[64,2048]{1,0:T(8,128)} %get-tuple-element.398, pred[]{:T(512)S(6)} %compare.19), kind=kOutput, calls=%fused_computation.61.clone.1 | convolution fusion | flops 2416181248 | bytes 7733761 | tf_op jit(solution)/shard_map/while/body/eval_jaxpr/gjr,gjm->rm/dot_general | solution.py:99
  508.7 1.9 broadcast_multiply_fusion
  510.6 0.0 reduce-scatter.2.cloned.1.call-update
  510.7 4.9 convolution_bitcast_fusion
  515.6 3.8 fusion.94
  519.4 38.7 %psum.7 = f32[64,64]{0,1:T(8,128)S(1)} all-reduce(f32[64,64]{0,1:T(8,128)S(1)} %fusion.94), channel_id=1, replica_groups=mesh['freq'=16,'mz'=2] {'freq','mz'}, use_global_device_ids=true, to_apply=%region_0.1 | all-reduce | flops 4096 | bytes 32768 | tf_op jit(solution)/shard_map/psum | solution.py:120
  558.1 0.1 copy.29
  558.2 5.8 %cholesky.16 = f32[64,64]{1,0:T(8,128)S(1)} custom-call(f32[64,64]{1,0:T(8,128)S(1)} %fusion.186), custom_call_target="Cholesky" | custom-call | tf_op jit(solution)/shard_map/jit(cholesky)/cholesky | solution.py:16
  564.1 0.6 compare_reduce_fusion
  564.8 0.7 fusion.181
  565.4 4.9 custom-call.8
  570.3 0.0 reduce-scatter.2.cloned.1.call-done
  570.4 1.0 fusion.184
  571.4 0.8 fusion.182
  (33 shorter events, 0.1 us)
Async XLA Ops:
  6.5 63.2 %all-gather.3.cloned.1.call-start = ((), (), s32[]{:S(2)}) async-start(), calls=%async_computation.2 | async-start | bytes 2162688 | tf_op jit(solution)/shard_map/all_gather | solution.py:38
  7.3 563.1 %reduce-scatter.2.cloned.1.call-start = ((), (), s32[]{:S(2)}) async-start(), calls=%async_computation.1 | async-start | bytes 557056 | tf_op jit(solution)/shard_map/reduce_scatter | solution.py:125
  164.0 53.2 %copy-start.2 = (s32[6144]{0:T(1024)}, s32[6144]{0:T(1024)S(1)}, u32[]{:S(2)}) copy-start(s32[6144]{0:T(1024)S(1)} %mul.1890) | copy-start | bytes 73732 | tf_op jit(solution)/shard_map/while
  217.2 36.9 %copy-start = (f32[8,8,16,384]{3,1,2,0:T(8,128)S(1)}, f32[8,8,16,384]{3,1,2,0:T(8,128)}, u32[]{:S(2)}) copy-start(f32[8,8,16,384]{3,1,2,0:T(8,128)} %copy.55) | copy-start | bytes 4718596 | tf_op jit(solution)/shard_map/while
  217.2 36.9 %copy-start.1 = (f32[8,8,16,384]{3,1,2,0:T(8,128)S(1)}, f32[8,8,16,384]{3,1,2,0:T(8,128)}, u32[]{:S(2)}) copy-start(f32[8,8,16,384]{3,1,2,0:T(8,128)} %copy.56) | copy-start | bytes 4718596 | tf_op jit(solution)/shard_map/while
  354.3 53.4 %copy-start.2 = (s32[6144]{0:T(1024)}, s32[6144]{0:T(1024)S(1)}, u32[]{:S(2)}) copy-start(s32[6144]{0:T(1024)S(1)} %mul.1890) | copy-start | bytes 73732 | tf_op jit(solution)/shard_map/while
  407.6 36.6 %copy-start = (f32[8,8,16,384]{3,1,2,0:T(8,128)S(1)}, f32[8,8,16,384]{3,1,2,0:T(8,128)}, u32[]{:S(2)}) copy-start(f32[8,8,16,384]{3,1,2,0:T(8,128)} %copy.55) | copy-start | bytes 4718596 | tf_op jit(solution)/shard_map/while
  407.7 36.6 %copy-start.1 = (f32[8,8,16,384]{3,1,2,0:T(8,128)S(1)}, f32[8,8,16,384]{3,1,2,0:T(8,128)}, u32[]{:S(2)}) copy-start(f32[8,8,16,384]{3,1,2,0:T(8,128)} %copy.56) | copy-start | bytes 4718596 | tf_op jit(solution)/shard_map/while
  508.7 6.9 %copy-start.3 = (f32[384]{0:T(512)S(1)}, f32[384]{0:T(512)}, u32[]{:S(2)}) copy-start(f32[384]{0:T(512)} %dynamic-slice_reduce_fusion) | copy-start | bytes 4612
  508.7 6.9 %copy-start.4 = (s32[384]{0:T(512)S(1)}, s32[384]{0:T(512)}, u32[]{:S(2)}) copy-start(s32[384]{0:T(512)} %broadcast_add_fusion) | copy-start | bytes 4612
  508.7 6.9 %copy-start.5 = (s32[4,64]{1,0:T(4,128)S(1)}, s32[4,64]{1,0:T(4,128)}, u32[]{:S(2)}) copy-start(s32[4,64]{1,0:T(4,128)} %constant_dynamic-slice_fusion) | copy-start | bytes 3076
  508.7 6.9 %copy-start.6 = (f32[4,64]{1,0:T(4,128)S(1)}, f32[4,64]{1,0:T(4,128)}, u32[]{:S(2)}) copy-start(f32[4,64]{1,0:T(4,128)} %constant_dynamic-slice_fusion.1) | copy-start | bytes 3076
  508.7 6.9 %copy-start.7 = (f32[384,64]{0,1:T(8,128)S(1)}, f32[384,64]{0,1:T(8,128)}, u32[]{:S(2)}) copy-start(f32[384,64]{0,1:T(8,128)} %fusion.92) | copy-start | bytes 294916
  508.7 6.9 %copy-start.8 = (f32[384,64]{0,1:T(8,128)S(1)}, f32[384,64]{0,1:T(8,128)}, u32[]{:S(2)}) copy-start(f32[384,64]{0,1:T(8,128)} %fusion.93) | copy-start | bytes 294916
Sparse Core Ops, SparseCore 0:
  10.5 59.1 all-gather.2
  510.8 54.7 reduce-scatter.1
where the time goes:
time: 582 us; the launch traced here: 579 us
  matrix products  271 us (47%)
  other arithmetic  166 us (29%)
  waiting for transfers between devices  56.8 us (10%)
  blocking collectives  38.7 us (7%)
  local copies, waits for them, and re-layouts  23.4 us (4%)
  between operations  13.9 us (2%)
  loops' own time  8.77 us (2%)
    dot_general x2, matrix products, fold_scans(): jnp.einsum('gfr,fj->gjr', flat_im, sin_scan, precision=PRECISE)  106 us
    dot_general x2, matrix products, fold_scans(): jnp.einsum('gfr,fj->gjr', flat_re, cos_scan, precision=PRECISE)  100 us
    dot_general x2, other arithmetic, fold_scans(): jnp.einsum('gfr,fj->gjr', flat_im, sin_scan, precision=PRECISE)  78 us
    dot_general x2, other arithmetic, fold_scans(): jnp.einsum('gfr,fj->gjr', flat_re, cos_scan, precision=PRECISE)  73.4 us
    all_gather x1, waiting for transfers between devices, on_device(): full_elution = lax.all_gather(elution, ('freq', 'mz'), axis=0, tiled=True)  56 us
    psum x1, blocking collectives, on_device(): lax.psum(jnp.einsum('kbr,kbs->rs', weights_col * model_re, model_re, prec...  38.7 us
    dot_general x2, matrix products, fold_scans(): jnp.einsum('gjr,gjm->rm', kernel, block_data.astype(jnp.float32), precisi...  12.7 us
  transfers between devices with their start and end apart: 2, of which 1 were waited for; matrix products, arithmetic and copies ran while one was open for 5% of the time, Pallas kernels for 0%

commit v1 on v0

v1 whole, which is shorter than its diff:
```python
import functools
import math

import jax
import jax.numpy as jnp
import numpy as np
from jax import lax
from jax.experimental import pallas as pl
from jax.experimental.pallas import tpu as pltpu
from jax.sharding import PartitionSpec as P

PRECISE = lax.Precision.HIGHEST
LANES = 128
REACH = 256
MIB = 1024 * 1024


def f32_dot(a, b, dims=(((1,), (0,)), ((), ()))):
    return lax.dot_general(a, b, dims, precision=PRECISE, preferred_element_type=jnp.float32)


def two_terms(x):
    high = x.astype(jnp.bfloat16)
    low = (x - high.astype(jnp.float32)).astype(jnp.bfloat16)
    return high, low


def vmem(count):
    return [pl.BlockSpec(memory_space=pltpu.VMEM)] * count


def pack_kernel(x_ref, o_ref):
    high, low = two_terms(x_ref[...])
    o_ref[...] = jnp.concatenate([high, low], axis=1)


def pack(elution):
    rows, components = elution.shape
    return pl.pallas_call(
        pack_kernel,
        out_shape=jax.ShapeDtypeStruct((rows, 2 * components), jnp.bfloat16),
        in_specs=vmem(1),
        out_specs=vmem(1)[0],
        name="pack_elution",
    )(elution)


def circulant_kernel(w_ref, lane_ref, twid_ref, row_ref, u_ref):
    rows = w_ref.shape[1]
    w = w_ref[...]
    over_lanes = (((0,), (0,)), ((), ()))
    a_re = f32_dot(w, lane_ref[0], over_lanes)
    a_im = -f32_dot(w, lane_ref[1], over_lanes)
    b_re = a_re * twid_ref[0] + a_im * twid_ref[1]
    b_im = a_im * twid_ref[0] - a_re * twid_ref[1]
    c = f32_dot(row_ref[0], b_re) + f32_dot(row_ref[1], b_im)
    sub = lax.broadcasted_iota(jnp.int32, (LANES, LANES), 0)
    lane = lax.broadcasted_iota(jnp.int32, (LANES, LANES), 1)

    def turned(row):
        return pltpu.roll(jnp.broadcast_to(c[row : row + 1], (LANES, LANES)), 0, 1, stride=1, stride_axis=0)

    before = turned(rows - 1)
    for row in range(rows):
        now = turned(row)
        high, low = two_terms(jnp.where(lane >= sub, now, before))
        u_ref[0:LANES, row * LANES : (row + 1) * LANES] = high
        u_ref[LANES:, row * LANES : (row + 1) * LANES] = low
        before = now


def circulant(bin_weight):
    length = bin_weight.shape[0]
    rows = length // LANES

    def tables(a, b, period):
        angle = 2.0 * math.pi / period * ((a[:, None] * b[None, :]) % period)
        return np.stack([np.cos(angle), np.sin(angle)])

    lane_ids, row_ids = np.arange(LANES), np.arange(rows)
    lane_table = tables(lane_ids, lane_ids, LANES).astype(np.float32)
    twid_table = tables(row_ids, lane_ids, length).astype(np.float32)
    row_table = (tables(row_ids, row_ids, rows) / length).astype(np.float32)
    return pl.pallas_call(
        circulant_kernel,
        out_shape=jax.ShapeDtypeStruct((2 * LANES, length), jnp.bfloat16),
        in_specs=vmem(4),
        out_specs=vmem(1)[0],
        cost_estimate=pl.CostEstimate(flops=2_000_000_000, bytes_accessed=4 * MIB, transcendentals=0),
        name="circulant_block",
    )(bin_weight.reshape(LANES, rows), lane_table, twid_table, row_table)


def product_kernel(
    places, order, packed, i_ref, e_ref, u_ref, amp_ref, lag_ref, num_ref, gram_ref, wide, terms, held, sems
):
    run_count, bin_count, local_mz = i_ref.shape
    components = amp_ref.shape[0]
    length = u_ref.shape[1]
    chunk = held.shape[2] // sems.shape[0]
    chunks = sems.shape[0]
    copies = []
    for n in range(chunks):
        part = pl.ds(n * chunk, chunk)
        copies.append(pltpu.make_async_copy(i_ref.at[:, :, part], held.at[:, :, part], sems.at[n]))
        copies[-1].start()

    freq_rank = lax.axis_index("freq")
    me = freq_rank * lax.axis_size("mz") + lax.axis_index("mz")
    start = lax.rem(freq_rank * bin_count + length - REACH, length)
    step = math.gcd(math.gcd(bin_count, LANES), e_ref.shape[1])
    per_shard = e_ref.shape[1] // step
    steps = length // step

    def bring(j, carry):
        at = lax.rem(start // step + j, steps)
        shard = at // per_shard
        if order is not None:
            turned = lax.bitwise_xor(shard, me)
            place = 0
            for bit, value in enumerate(order):
                place = place + (lax.rem(turned // value, 2) << bit)
            shard = place
        row = pl.multiple_of(lax.rem(at, per_shard) * step, step)
        block = e_ref[pl.ds(shard, 1), pl.ds(row, step), :][0]
        to = pl.multiple_of(j * step, step)
        wide[pl.ds(to + LANES, step), 0:LANES] = block
        wide[pl.ds(to, step), LANES:] = block
        return carry

    extra = (wide.shape[0] - length) // step
    lax.fori_loop(0, steps + extra - LANES // step, bring, 0)

    u = u_ref[...]
    pieces, windows = [], []
    for a in range(0, places, 2):
        rows = wide[LANES + a * LANES : LANES + a * LANES + length, :]
        made = lax.dot_general(
            u, rows, (((1,), (0,)), ((), ())), preferred_element_type=jnp.float32
        )
        made = made[:LANES] + made[LANES:]
        for half in range(min(2, places - a)):
            piece = made[:, half * LANES : (half + 1) * LANES].T
            pieces.append(piece[:components] + piece[components:])
    for a in range(places):
        piece = wide[LANES + a * LANES : 2 * LANES + a * LANES, 0:LANES].astype(jnp.float32).T
        windows.append(piece[:components] + piece[components:])
    base = jnp.concatenate(
        [jnp.concatenate(pieces, axis=1), jnp.concatenate(windows, axis=1)], axis=0
    )
    span = -(-bin_count // LANES) * LANES
    for k in range(run_count):
        lag = lag_ref[:, k : k + 1]
        left = REACH - 1 - jnp.concatenate([lag, lag], axis=0)
        y = base
        for bit in (7, 6, 5, 4, 3, 2, 1, 0):
            move = 1 << bit
            y = jnp.where(
                lax.rem(left // move, 2) == 1, pltpu.roll(y, y.shape[1] - move, 1), y
            )
            if move == LANES:
                y = y[:, : span + LANES]
        y = pltpu.roll(y, y.shape[1] - 1, 1)[:, :bin_count]
        amp = amp_ref[:, k : k + 1]
        high, low = two_terms(y * jnp.concatenate([amp, amp], axis=0))
        terms[0:components, k * bin_count : (k + 1) * bin_count] = high[:components]
        terms[components : 2 * components, k * bin_count : (k + 1) * bin_count] = low[:components]
        terms[2 * components : 3 * components, k * bin_count : (k + 1) * bin_count] = high[components:]
        terms[3 * components :, k * bin_count : (k + 1) * bin_count] = low[components:]
    model = terms[0 : 2 * components, :]
    gram = lax.dot_general(
        model, terms[2 * components :, :], (((1,), (1,)), ((), ())), preferred_element_type=jnp.float32
    )
    gram = gram[:components] + gram[components:]
    gram = gram[:, :components] + gram[:, components:]
    if packed:
        half = components // 2
        gram = jnp.concatenate([gram[:half], gram[half:]], axis=1)
        for n in range(num_ref.shape[0]):
            num_ref[n, components:, :] = gram
    gram_ref[...] = gram

    for n in range(chunks):
        copies[n].wait()
        data = held[:, :, n * chunk : (n + 1) * chunk].reshape(run_count * bin_count, chunk)
        made = jnp.dot(model, data, preferred_element_type=jnp.float32)
        made = made[:components] + made[components:]
        if packed:
            for part in range(chunk // LANES):
                num_ref[n * (chunk // LANES) + part, 0:components, :] = made[
                    :, part * LANES : (part + 1) * LANES
                ]
        else:
            num_ref[:, n * chunk : (n + 1) * chunk] = made


def product(intensity, gathered, order, u, loadings, shifts, packed):
    run_count, bin_count, local_mz = intensity.shape
    components = loadings.shape[1]
    length = u.shape[1]
    places = -(-(bin_count + REACH) // LANES)
    chunk = 256
    num_shape = (local_mz // LANES, components + components // 2, LANES) if packed else (components, local_mz)
    gram_shape = (components // 2, LANES) if packed else (components, components)
    scratch_rows = LANES + length + 2 * LANES * ((places - 1) // 2)
    return pl.pallas_call(
        functools.partial(product_kernel, places, order, packed),
        out_shape=(
            jax.ShapeDtypeStruct(num_shape, jnp.float32),
            jax.ShapeDtypeStruct(gram_shape, jnp.float32),
        ),
        in_specs=[pl.BlockSpec(memory_space=pl.ANY)] + vmem(4),
        out_specs=tuple(vmem(2)),
        scratch_shapes=[
            pltpu.VMEM((scratch_rows, 2 * LANES), jnp.bfloat16),
            pltpu.VMEM((4 * components, run_count * bin_count), jnp.bfloat16),
            pltpu.VMEM(intensity.shape, jnp.bfloat16),
            pltpu.SemaphoreType.DMA((local_mz // chunk,)),
        ],
        compiler_params=pltpu.CompilerParams(vmem_limit_bytes=48 * MIB),
        cost_estimate=pl.CostEstimate(
            flops=8_000_000_000, bytes_accessed=2 * intensity.size, transcendentals=0
        ),
        name="model_products",
    )(intensity, gathered, u, loadings.T, shifts.T)


def eliminate(gram, right):
    components = gram.shape[0]
    row_id = lax.broadcasted_iota(jnp.int32, (components, 1), 0)
    for j in range(components):
        pivot = 1.0 / gram[j : j + 1, j : j + 1]
        factor = jnp.where(row_id == j, 0.0, gram[:, j : j + 1] * pivot)
        gram, right = gram - factor * gram[j : j + 1, :], right - factor * right[j : j + 1, :]
    eye = row_id == lax.broadcasted_iota(jnp.int32, gram.shape, 1)
    return right / jnp.sum(jnp.where(eye, gram, 0.0), axis=1, keepdims=True)


def solve_packed_kernel(x_ref, o_ref):
    components = o_ref.shape[0]
    half = components // 2
    total = x_ref[0]
    for n in range(1, x_ref.shape[0]):
        total = total + x_ref[n]
    tail = total[components:]
    gram = jnp.concatenate([tail[:, :components], tail[:, components:]], axis=0)
    o_ref[...] = eliminate(gram, total[:components])


def solve_kernel(g_ref, n_ref, o_ref):
    o_ref[...] = eliminate(g_ref[...], n_ref[...])


def solve_call(kernel, out_shape, *args):
    return pl.pallas_call(
        kernel,
        out_shape=jax.ShapeDtypeStruct(out_shape, jnp.float32),
        in_specs=vmem(len(args)),
        out_specs=vmem(1)[0],
        compiler_params=pltpu.CompilerParams(vmem_limit_bytes=32 * MIB),
        name="solve",
    )(*args)


def doubling_gather(mine, axes, count, order):
    held = mine[None]
    for value in order:
        came = lax.ppermute(held, axes, [(i, i ^ value) for i in range(count)])
        held = jnp.concatenate([held, came], axis=0)
    return held


def on_device(intensity, elution, loadings, shifts, bin_weight):
    freq_count = lax.axis_size("freq")
    mz_count = lax.axis_size("mz")
    count = freq_count * mz_count
    components = loadings.shape[1]
    axes = ("freq", "mz")
    mine = pack(elution)
    own = intensity.shape[2] // freq_count
    packed = own == LANES and 2 * components == LANES
    order = None
    if count & (count - 1) == 0 and elution.shape[0] % 64 == 0:
        bits = [1 << b for b in range(count.bit_length() - 1)]
        order = tuple(bits[::-1][: len(bits) - 2] + [bits[0], bits[1]])
        gathered = doubling_gather(mine, axes, count, order)
    else:
        gathered = lax.all_gather(mine, axes, axis=0).reshape(-1, math.gcd(intensity.shape[1], LANES), LANES)
    u = circulant(bin_weight)
    numerator, gram = product(intensity, gathered, order, u, loadings, shifts, packed)
    if packed:
        spread = lax.all_to_all(numerator, "freq", 0, 0)
        return solve_call(solve_packed_kernel, (components, own), spread)
    gram = lax.psum(gram, "freq")
    owned = lax.psum_scatter(numerator, "freq", scatter_dimension=1, tiled=True)
    return solve_call(solve_kernel, (components, own), gram, owned)


def solution(mesh):
    in_specs = (P(None, "freq", "mz"), P(("freq", "mz"), None), P(), P(), P())
    out_specs = P(None, ("mz", "freq"))
    return jax.shard_map(on_device, mesh=mesh, in_specs=in_specs, out_specs=out_specs, check_vma=False)
```

time: 582 us -> 90.9 us (0.16)
  matrix products: 271 us -> 0 us
  other arithmetic: 166 us -> 2.47 us
  waiting for transfers between devices: 56.8 us -> 15.1 us
  Pallas kernels: 0 us -> 31.4 us
  local copies, waits for them, and re-layouts: 23.4 us -> 5.6 us
  between operations: 13.9 us -> 0.11 us
  blocking collectives: 38.7 us -> 26.3 us
  starting transfers between devices: 0.04 us -> 9.12 us
  loops' own time: 8.77 us -> 0 us
    dot_general x20 -> x0, matrix products: 269 us -> none  [the longest x2 106 us: fold_scans(): jnp.einsum('gfr,fj->gjr', flat_im, sin_scan, precision=PRECISE)]
    dot_general x4 -> x0, other arithmetic: 151 us -> none  [the longest x2 78 us: fold_scans(): jnp.einsum('gfr,fj->gjr', flat_im, sin_scan, precision=PRECISE)]
    all_gather x1 -> x0, waiting for transfers between devices: 56 us -> none  [on_device(): full_elution = lax.all_gather(elution, ('freq', 'mz'), axis=0, tiled=True)]
    psum x1 -> x0, blocking collectives: 38.7 us -> none  [on_device(): lax.psum(jnp.einsum('kbr,kbs->rs', weights_col * model_re, model_re, prec...]
    pallas_call x0 -> x4, Pallas kernels: none -> 31.4 us  [the longest x1 19.7 us: product(): pl.pallas_call(functools.partial(product_kernel, places, order, packed),...]
    all_to_all x0 -> x1, blocking collectives: none -> 26.3 us  [on_device(): spread = lax.all_to_all(numerator, 'freq', 0, 0)]
    ppermute x0 -> x5, waiting for transfers between devices: none -> 15.1 us  [doubling_gather(): came = lax.ppermute(held, axes, [(i, i ^ value) for i in range(count)])]
    another operation x5 -> x0, other arithmetic: 12.1 us -> none  [the longest x3 6.52 us: cholesky_solve(): factor = jnp.linalg.cholesky(gram_matrix)]
  transfers between devices with their start and end apart: 2 -> 5, of which waited for: 1 -> 4; matrix products, arithmetic and copies ran while one was open for 5% -> 2% of each run, Pallas kernels for 0% -> 4%
where the time goes in v1:
time: 90.9 us; the launch traced here: 90 us
  Pallas kernels  31.4 us (35%)
  blocking collectives  26.3 us (29%)
  waiting for transfers between devices  15.1 us (17%)
  starting transfers between devices  9.12 us (10%)
  local copies, waits for them, and re-layouts  5.6 us (6%)
  other arithmetic  2.47 us (3%)
    all_to_all x1, blocking collectives, on_device(): spread = lax.all_to_all(numerator, 'freq', 0, 0)  26.3 us
    pallas_call x1, Pallas kernels, product(): pl.pallas_call(functools.partial(product_kernel, places, order, packed),...  19.7 us
    ppermute x5, waiting for transfers between devices, doubling_gather(): came = lax.ppermute(held, axes, [(i, i ^ value) for i in range(count)])  15.1 us
    ppermute x5, starting transfers between devices, doubling_gather(): came = lax.ppermute(held, axes, [(i, i ^ value) for i in range(count)])  9.12 us
    pallas_call x1, Pallas kernels, solve_call(): pl.pallas_call(kernel, out_shape=jax.ShapeDtypeStruct(out_shape, jnp.floa...  6.08 us
    unnamed x15, local copies, waits for them, and re-layouts  4.59 us
    pallas_call x1, Pallas kernels, circulant(): pl.pallas_call(circulant_kernel, out_shape=jax.ShapeDtypeStruct((2 * LANE...  4.01 us
    concatenate x3, other arithmetic, doubling_gather(): held = jnp.concatenate([held, came], axis=0)  2.47 us
  transfers between devices with their start and end apart: 5, of which 4 were waited for; matrix products, arithmetic and copies ran while one was open for 2% of the time, Pallas kernels for 4%

profile of v1, /device:TPU:0, one launch (start us, length us, event | category | flops | bytes accessed | tf_op | source)
XLA Modules:
  0.0 90.0 jit_solution(17213563579180055696)
XLA Ops:
  0.0 1.6 %copy.12.x_ref = f32[192,64]{1,0:T(8,128)} copy(f32[192,64]{0,1:T(8,128)} %param.9) | data formatting | bytes 98304 | tf_op args[1]
  1.6 1.6 %pack_elution.1 = bf16[192,128]{1,0:T(8,128)(2,1)} custom-call(f32[192,64]{1,0:T(8,128)} %copy.12.x_ref), custom_call_target="tpu_custom_call" | custom-call | tf_op jit(solution)/shard_map/pack_elution/pallas_call | solution.py:39
  3.2 4.0 %collective-permute-start = (bf16[1,192,128]{2,1,0:T(8,128)(2,1)}, bf16[1,192,128]{2,1,0:T(8,128)(2,1)S(1)}, u32[]{:S(2)}, u32[]{:S(2)}) collective-permute-start(bf16[1,192,128]{2,1,0:T(8,128)(2,1)} %bitcast.7), channel_id=1, source_target_pairs={{0,16},{1,17},{2,18},{3,19},{4,20},{5,21},{6,22},{7,23},{8,24},{9,... | collective-permute-start | bytes 147464 | tf_op jit(solution)/shard_map/ppermute | solution.py:268
  7.2 2.8 %collective-permute-done = bf16[1,192,128]{2,1,0:T(8,128)(2,1)S(1)} collective-permute-done((bf16[1,192,128]{2,1,0:T(8,128)(2,1)}, bf16[1,192,128]{2,1,0:T(8,128)(2,1)S(1)}, u32[]{:S(2)}, u32[]{:S(2)}) %collective-permute-start) | collective-permute-done | bytes 49184 | tf_op jit(solution)/shard_map/ppermute | solution.py:268
  10.0 0.8 pad_maximum_fusion.2
  10.8 1.4 %collective-permute-start.1 = (bf16[2,192,128]{2,1,0:T(8,128)(2,1)S(1)}, bf16[2,192,128]{2,1,0:T(8,128)(2,1)S(1)}, u32[]{:S(2)}, u32[]{:S(2)}) collective-permute-start(bf16[2,192,128]{2,1,0:T(8,128)(2,1)S(1)} %pad_maximum_fusion.2), channel_id=1, source_target_pairs={{0,8},{1,9},{2,10},{3,11},{4,12},{5,13},{6,14},{7,15},{8,0},{9,1},... | collective-permute-start | bytes 294920 | tf_op jit(solution)/shard_map/ppermute | solution.py:268
  12.3 3.2 %collective-permute-done.1 = bf16[2,192,128]{2,1,0:T(8,128)(2,1)S(1)} collective-permute-done((bf16[2,192,128]{2,1,0:T(8,128)(2,1)S(1)}, bf16[2,192,128]{2,1,0:T(8,128)(2,1)S(1)}, u32[]{:S(2)}, u32[]{:S(2)}) %collective-permute-start.1) | collective-permute-done | bytes 98336 | tf_op jit(solution)/shard_map/ppermute | solution.py:268
  15.5 0.8 pad_maximum_fusion.1
  16.3 0.0 copy-start.2
  16.3 0.0 copy-start.3
  16.3 0.0 copy-start.1
  16.4 1.8 %collective-permute-start.2 = (bf16[4,192,128]{2,1,0:T(8,128)(2,1)S(1)}, bf16[4,192,128]{2,1,0:T(8,128)(2,1)S(1)}, u32[]{:S(2)}, u32[]{:S(2)}) collective-permute-start(bf16[4,192,128]{2,1,0:T(8,128)(2,1)S(1)} %pad_maximum_fusion.1), channel_id=1, source_target_pairs={{0,4},{1,5},{2,6},{3,7},{4,0},{5,1},{6,2},{7,3},{8,12},{9,13},{10,... | collective-permute-start | bytes 589832 | tf_op jit(solution)/shard_map/ppermute | solution.py:268
  18.1 4.0 %collective-permute-done.2 = bf16[4,192,128]{2,1,0:T(8,128)(2,1)S(1)} collective-permute-done((bf16[4,192,128]{2,1,0:T(8,128)(2,1)S(1)}, bf16[4,192,128]{2,1,0:T(8,128)(2,1)S(1)}, u32[]{:S(2)}, u32[]{:S(2)}) %collective-permute-start.2) | collective-permute-done | bytes 196640 | tf_op jit(solution)/shard_map/ppermute | solution.py:268
  22.1 0.8 pad_maximum_fusion
  22.9 1.8 %collective-permute-start.3 = (bf16[8,192,128]{2,1,0:T(8,128)(2,1)S(1)}, bf16[8,192,128]{2,1,0:T(8,128)(2,1)S(1)}, u32[]{:S(2)}, u32[]{:S(2)}) collective-permute-start(bf16[8,192,128]{2,1,0:T(8,128)(2,1)S(1)} %pad_maximum_fusion), channel_id=1, source_target_pairs={{0,1},{1,0},{2,3},{3,2},{4,5},{5,4},{6,7},{7,6},{8,9},{9,8},{10,11... | collective-permute-start | bytes 1179656 | tf_op jit(solution)/shard_map/ppermute | solution.py:268
  24.7 0.8 constant_dynamic-update-slice_fusion.4
  25.6 0.1 constant_dynamic-update-slice_fusion.1
  25.7 5.1 %collective-permute-done.3 = bf16[8,192,128]{2,1,0:T(8,128)(2,1)S(1)} collective-permute-done((bf16[8,192,128]{2,1,0:T(8,128)(2,1)S(1)}, bf16[8,192,128]{2,1,0:T(8,128)(2,1)S(1)}, u32[]{:S(2)}, u32[]{:S(2)}) %collective-permute-start.3) | collective-permute-done | bytes 393248 | tf_op jit(solution)/shard_map/ppermute | solution.py:268
  30.8 0.2 constant_dynamic-update-slice_fusion
  31.0 0.1 collective-permute-start.4
  31.1 0.0 copy-done.2
  31.1 0.1 copy.13
  31.2 0.0 copy-done.3
  31.2 0.1 copy.14
  31.2 0.0 copy-done.1
  31.2 0.7 reshape.3.w_ref
  31.9 4.0 %circulant_block.1.u_ref = bf16[256,6144]{1,0:T(8,128)(2,1)} custom-call(f32[128,48]{1,0:T(8,128)} %reshape.3.w_ref, f32[2,128,128]{2,1,0:T(8,128)} %constant.6.clone.lane_ref, f32[2,48,128]{2,1,0:T(8,128)} %constant.7.clone.twid_ref, f32[2,48,48]{2,1,0:T(8,128)} %constant.8.clone.row_ref), custom_call_target="tpu_custom_call" | custom-call | flops 2000000000 | bytes 4194304 | tf_op jit(solution)/shard_map/circulant_block/pallas_call | solution.py:84
  36.0 0.0 collective-permute-done.4
  36.0 0.1 constant_dynamic-update-slice_fusion.5.e_ref
  36.1 0.0 copy-start
  36.1 1.9 %copy-done = bf16[256,6144]{1,0:T(8,128)(2,1)S(1)} copy-done((bf16[256,6144]{1,0:T(8,128)(2,1)S(1)}, bf16[256,6144]{1,0:T(8,128)(2,1)}, u32[]{:S(2)}) %copy-start) | copy-done | bytes 3145752
  38.0 19.7 %model_products.1 = (f32[16,96,128]{2,1,0:T(8,128)S(1)}, f32[32,128]{1,0:T(8,128)}) custom-call(bf16[8,384,2048]{2,1,0:T(8,128)(2,1)} %i_ref.1, bf16[32,192,128]{2,1,0:T(8,128)(2,1)S(1)} %constant_dynamic-update-slice_fusion.5.e_ref, bf16[256,6144]{1,0:T(8,128)(2,1)S(1)} %copy-done, f32[64,8]{1,0:T(8,128)S(1)} %bitcast.5, s32[64,8]{1,0:T(8,128)S(1)} %bitcast.6), custom_call_target="tpu_custom_call" | custom-call | flops 8000000000 | bytes 12582912 | tf_op jit(solution)/shard_map/model_products/pallas_call | solution.py:206
  57.7 26.3 %all_to_all.5.x_ref = f32[16,96,128]{2,1,0:T(8,128)S(1)} all-to-all(f32[16,96,128]{2,1,0:T(8,128)S(1)} %get-tuple-element.6), channel_id=1, replica_groups=mesh['freq'=16,'mz'=2] {'freq'}, dimensions={0} | all-to-all | bytes 1572864 | tf_op jit(solution)/shard_map/all_to_all | solution.py:292
  84.0 6.1 %solve.1 = f32[64,128]{1,0:T(8,128)} custom-call(f32[16,96,128]{2,1,0:T(8,128)S(1)} %all_to_all.5.x_ref), custom_call_target="tpu_custom_call" | custom-call | tf_op jit(solution)/shard_map/solve/pallas_call | solution.py:255
  (2 shorter events, 0.1 us)
Async XLA Ops:
  3.2 6.8 %collective-permute-start = (bf16[1,192,128]{2,1,0:T(8,128)(2,1)}, bf16[1,192,128]{2,1,0:T(8,128)(2,1)S(1)}, u32[]{:S(2)}, u32[]{:S(2)}) collective-permute-start(bf16[1,192,128]{2,1,0:T(8,128)(2,1)} %bitcast.7), channel_id=1, source_target_pairs={{0,16},{1,17},{2,18},{3,19},{4,20},{5,21},{6,22},{7,23},{8,24},{9,... | collective-permute-start | bytes 147464 | tf_op jit(solution)/shard_map/ppermute | solution.py:268
  10.8 4.7 %collective-permute-start.1 = (bf16[2,192,128]{2,1,0:T(8,128)(2,1)S(1)}, bf16[2,192,128]{2,1,0:T(8,128)(2,1)S(1)}, u32[]{:S(2)}, u32[]{:S(2)}) collective-permute-start(bf16[2,192,128]{2,1,0:T(8,128)(2,1)S(1)} %pad_maximum_fusion.2), channel_id=1, source_target_pairs={{0,8},{1,9},{2,10},{3,11},{4,12},{5,13},{6,14},{7,15},{8,0},{9,1},... | collective-permute-start | bytes 294920 | tf_op jit(solution)/shard_map/ppermute | solution.py:268
  16.3 14.7 %copy-start.2 = (f32[8,64]{1,0:T(8,128)S(1)}, f32[8,64]{1,0:T(8,128)}, u32[]{:S(2)}) copy-start(f32[8,64]{1,0:T(8,128)} %param.10) | copy-start | bytes 6148
  16.3 14.8 %copy-start.3 = (s32[8,64]{1,0:T(8,128)S(1)}, s32[8,64]{1,0:T(8,128)}, u32[]{:S(2)}) copy-start(s32[8,64]{1,0:T(8,128)} %param.11) | copy-start | bytes 6148
  16.3 14.9 %copy-start.1 = (f32[6144]{0:T(1024)S(1)}, f32[6144]{0:T(1024)}, u32[]{:S(2)}) copy-start(f32[6144]{0:T(1024)} %param.12) | copy-start | bytes 73732
  16.4 5.7 %collective-permute-start.2 = (bf16[4,192,128]{2,1,0:T(8,128)(2,1)S(1)}, bf16[4,192,128]{2,1,0:T(8,128)(2,1)S(1)}, u32[]{:S(2)}, u32[]{:S(2)}) collective-permute-start(bf16[4,192,128]{2,1,0:T(8,128)(2,1)S(1)} %pad_maximum_fusion.1), channel_id=1, source_target_pairs={{0,4},{1,5},{2,6},{3,7},{4,0},{5,1},{6,2},{7,3},{8,12},{9,13},{10,... | collective-permute-start | bytes 589832 | tf_op jit(solution)/shard_map/ppermute | solution.py:268
  22.9 7.8 %collective-permute-start.3 = (bf16[8,192,128]{2,1,0:T(8,128)(2,1)S(1)}, bf16[8,192,128]{2,1,0:T(8,128)(2,1)S(1)}, u32[]{:S(2)}, u32[]{:S(2)}) collective-permute-start(bf16[8,192,128]{2,1,0:T(8,128)(2,1)S(1)} %pad_maximum_fusion), channel_id=1, source_target_pairs={{0,1},{1,0},{2,3},{3,2},{4,5},{5,4},{6,7},{7,6},{8,9},{9,8},{10,11... | collective-permute-start | bytes 1179656 | tf_op jit(solution)/shard_map/ppermute | solution.py:268
  31.0 5.0 %collective-permute-start.4 = (bf16[16,192,128]{2,1,0:T(8,128)(2,1)S(1)}, bf16[16,192,128]{2,1,0:T(8,128)(2,1)S(1)}, u32[]{:S(2)}, u32[]{:S(2)}) collective-permute-start(bf16[16,192,128]{2,1,0:T(8,128)(2,1)S(1)} %get-tuple-element.7), channel_id=1, source_target_pairs={{0,2},{1,3},{2,0},{3,1},{4,6},{5,7},{6,4},{7,5},{8,10},{9,11},{10,... | collective-permute-start | bytes 2359304 | tf_op jit(solution)/shard_map/ppermute | solution.py:268
  36.1 1.9 %copy-start = (bf16[256,6144]{1,0:T(8,128)(2,1)S(1)}, bf16[256,6144]{1,0:T(8,128)(2,1)}, u32[]{:S(2)}) copy-start(bf16[256,6144]{1,0:T(8,128)(2,1)} %circulant_block.1.u_ref) | copy-start | bytes 9437188
